TPU v7x, 32 devices: a whole 2x2x4 slice. The times are simulated.
32 devices in a mesh: dp: 8 (over z, x), seq: 4 (over y, core).
Axes of the slice: x: 2, y: 2, z: 4, core: 2. Of those that a mesh axis runs over, the one named last changes fastest.
Arguments:
- inputs: bfloat16 [1024, 24, 512], P('seq', 'dp'), may hold values from -6 to 6
- cotangent: bfloat16 [1024, 24, 512], P('seq', 'dp'), may hold values from -6 to 6
- w_qkv: bfloat16 [2, 512, 1536], P(None, ('dp', 'seq')), may hold values from -0.25 to 0.25
- w_out: bfloat16 [2, 512, 512], P(None, ('dp', 'seq')), may hold values from -0.25 to 0.25
- w_up: bfloat16 [2, 512, 2048], P(None, ('dp', 'seq')), may hold values from -0.25 to 0.25
- w_down: bfloat16 [2, 2048, 512], P(None, ('dp', 'seq')), may hold values from -0.25 to 0.25
- norm_gains: bfloat16 [2, 1024], P(None, ('dp', 'seq')), may hold values from 0.5 to 1.5
- biases: bfloat16 [2, 5120], P(None, ('dp', 'seq')), may hold values from -1.75 to 1.75
- time_table: bfloat16 [2, 1000, 512], P(None, None, ('dp', 'seq')), may hold values from -6 to 6
- timesteps: int32 [24], P('dp'), may hold values from 0 to 999
- importance: float32 [1000], replicated, may hold values from 0.25 to 4
Outputs:
- activations: float32 [1024, 24, 512], P('seq', 'dp')
- input_grad: float32 [1024, 24, 512], P('seq', 'dp')
- grad_qkv: float32 [2, 512, 1536], P(None, ('dp', 'seq'))
- grad_out: float32 [2, 512, 512], P(None, ('dp', 'seq'))
- up_weight_gradient: float32 [2, 512, 2048], P(None, ('dp', 'seq'))
- down_weight_gradient: float32 [2, 2048, 512], P(None, ('dp', 'seq'))
- grad_gains: float32 [2, 1024], P(None, ('dp', 'seq'))
- grad_biases: float32 [2, 5120], P(None, ('dp', 'seq'))
- grad_table: float32 [2, 1000, 512], P(None, None, ('dp', 'seq'))
All inputs are finite; a program needn't handle non-finite values.
Results may differ from a plain program's by a relative error of at most 0.01.
Values may be sent and summed in bfloat16 or wider, within the bound.
A program may use at most 192 MiB of HBM per device.

v0:
```python
import functools
import math

import jax
import jax.numpy as jnp
from jax import lax
from jax.experimental import pallas as pl
from jax.experimental.pallas import tpu as pltpu
from jax.sharding import PartitionSpec as P

D = 512
HEADS = 8
HEAD_DIM = 64
FF = 2048
STEPS = 1000
LAYERS = 2


EPS = 1e-05
HIGH = lax.Precision.HIGHEST


def layer_norm(values, gain_vec, bias_vec):
    centered = values - jnp.mean(values, axis=-1, keepdims=True)
    spread = jnp.mean(centered * centered, axis=-1, keepdims=True)
    return centered * lax.rsqrt(spread + EPS) * gain_vec + bias_vec


def attend(queries, keys_all, values_all):
    row_count, seq_count, model_width = queries.shape
    score_scale = 1.0 / math.sqrt(HEAD_DIM)

    def per_seq(seq_index, loop_state):
        outputs, log_tot = loop_state
        query_per_head = lax.dynamic_index_in_dim(queries, seq_index, 1, keepdims=False).reshape(
            row_count, HEADS, HEAD_DIM
        )
        key_per_head = lax.dynamic_index_in_dim(keys_all, seq_index, 1, keepdims=False).reshape(
            -1, HEADS, HEAD_DIM
        )
        value_per_head = lax.dynamic_index_in_dim(values_all, seq_index, 1, keepdims=False).reshape(
            -1, HEADS, HEAD_DIM
        )
        scores = (
            jnp.einsum(
                "xsv,usv->sxu", query_per_head, key_per_head, preferred_element_type=jnp.float32
            )
            * score_scale
        )
        row_max = jnp.max(scores, axis=-1, keepdims=True)
        expon = jnp.exp(scores - row_max)
        summed = jnp.sum(expon, axis=-1, keepdims=True)
        attention_probability = (expon / summed).astype(jnp.bfloat16)
        attn_out = jnp.einsum(
            "gir,rgo->igo",
            attention_probability,
            value_per_head,
            preferred_element_type=jnp.float32,
        )
        attn_out = attn_out.astype(jnp.bfloat16).reshape(row_count, 1, model_width)
        outputs = lax.dynamic_update_slice_in_dim(outputs, attn_out, seq_index, 1)
        log_tot = lax.dynamic_update_slice_in_dim(
            log_tot, (row_max + jnp.log(summed))[None, :, :, 0], seq_index, 0
        )
        return (outputs, log_tot)

    start_state = (
        jnp.zeros(queries.shape, jnp.bfloat16),
        jnp.zeros((seq_count, HEADS, row_count), jnp.float32),
    )
    return lax.fori_loop(0, seq_count, per_seq, start_state)


def attend_back(queries, keys_all, values_all, log_tot, grad_attn):
    row_count, seq_count, model_width = queries.shape
    key_count = keys_all.shape[0]
    score_scale = 1.0 / math.sqrt(HEAD_DIM)

    def per_seq(seq_index, loop_state):
        grad_query, part_key, part_value = loop_state
        query_per_head = lax.dynamic_index_in_dim(queries, seq_index, 1, keepdims=False).reshape(
            row_count, HEADS, HEAD_DIM
        )
        key_per_head = lax.dynamic_index_in_dim(keys_all, seq_index, 1, keepdims=False).reshape(
            key_count, HEADS, HEAD_DIM
        )
        value_per_head = lax.dynamic_index_in_dim(values_all, seq_index, 1, keepdims=False).reshape(
            key_count, HEADS, HEAD_DIM
        )
        hidden_state_gradient = lax.dynamic_index_in_dim(
            grad_attn, seq_index, 1, keepdims=False
        ).reshape(row_count, HEADS, HEAD_DIM)
        log_seq = lax.dynamic_index_in_dim(log_tot, seq_index, 0, keepdims=False)
        scores = (
            jnp.einsum(
                "xsv,usv->sxu", query_per_head, key_per_head, preferred_element_type=jnp.float32
            )
            * score_scale
        )
        attn_f = jnp.exp(scores - log_seq[:, :, None])
        attention_probability = attn_f.astype(jnp.bfloat16)
        value_part = jnp.einsum(
            "uxo,xuc->ouc",
            attention_probability,
            hidden_state_gradient,
            preferred_element_type=jnp.float32,
        )
        probability_gradient = jnp.einsum(
            "xsv,usv->sxu",
            hidden_state_gradient,
            value_per_head,
            preferred_element_type=jnp.float32,
        )
        row_delta = jnp.sum(probability_gradient * attn_f, axis=-1, keepdims=True)
        score_gradient = (attn_f * (probability_gradient - row_delta)).astype(jnp.bfloat16)
        query_part = (
            jnp.einsum(
                "gir,rgo->igo", score_gradient, key_per_head, preferred_element_type=jnp.float32
            )
            * score_scale
        )
        key_part = (
            jnp.einsum(
                "uxo,xuc->ouc", score_gradient, query_per_head, preferred_element_type=jnp.float32
            )
            * score_scale
        )
        grad_query = lax.dynamic_update_slice_in_dim(
            grad_query, query_part.reshape(row_count, 1, model_width), seq_index, 1
        )
        part_key = lax.dynamic_update_slice_in_dim(
            part_key, key_part.reshape(key_count, 1, model_width), seq_index, 1
        )
        part_value = lax.dynamic_update_slice_in_dim(
            part_value, value_part.reshape(key_count, 1, model_width), seq_index, 1
        )
        return (grad_query, part_key, part_value)

    start_state = (
        jnp.zeros(queries.shape, jnp.float32),
        jnp.zeros(keys_all.shape, jnp.float32),
        jnp.zeros(keys_all.shape, jnp.float32),
    )
    return lax.fori_loop(0, seq_count, per_seq, start_state)


def forward_layer(hidden, fetched, onehot):
    mat_qkv, mat_out, up_matrix, down_matrix, gain_row, bias_row, time_rows = fetched
    gain_f = gain_row.astype(jnp.float32)
    bias_f = bias_row.astype(jnp.float32)
    seq_embed = jnp.dot(onehot.astype(jnp.bfloat16), time_rows, preferred_element_type=jnp.float32)
    summed_in = hidden + seq_embed[None]
    normed_one = layer_norm(summed_in, gain_f[:D], bias_f[4 * D + FF : 5 * D + FF]).astype(
        jnp.bfloat16
    )
    linear = jnp.dot(normed_one, mat_qkv, preferred_element_type=jnp.float32)
    queries = (linear[..., :D] + bias_f[:D]).astype(jnp.bfloat16)
    keys_loc = linear[..., D : 2 * D].astype(jnp.bfloat16)
    values_loc = (linear[..., 2 * D :] + bias_f[D : 2 * D]).astype(jnp.bfloat16)
    keys_all, values_all = (
        lax.all_gather(keys_loc, "seq", axis=0, tiled=True),
        lax.all_gather(values_loc, "seq", axis=0, tiled=True),
    )
    attn_out, log_tot = attend(queries, keys_all, values_all)
    after_attn = (
        summed_in
        + jnp.dot(attn_out, mat_out, preferred_element_type=jnp.float32)
        + bias_f[2 * D : 3 * D]
    )
    second_normalized = layer_norm(after_attn, gain_f[D:], bias_f[5 * D + FF :]).astype(
        jnp.bfloat16
    )
    upward = (
        jnp.dot(second_normalized, up_matrix, preferred_element_type=jnp.float32)
        + bias_f[3 * D : 3 * D + FF]
    )
    gelu_output = jax.nn.gelu(upward).astype(jnp.bfloat16)
    result = (
        after_attn
        + jnp.dot(gelu_output, down_matrix, preferred_element_type=jnp.float32)
        + bias_f[3 * D + FF : 4 * D + FF]
    )
    record = (
        summed_in,
        normed_one,
        queries,
        keys_loc,
        values_loc,
        attn_out,
        log_tot,
        after_attn,
        second_normalized,
        upward,
        gelu_output,
        keys_all,
        values_all,
    )
    return (result, record)


def backward_layer(hidden_state_gradient, fetched, record, onehot, kv_pair):
    mat_qkv = fetched[0]
    mat_out = fetched[1]
    up_matrix = fetched[2]
    down_matrix = fetched[3]
    gain_f = fetched[4].astype(jnp.float32)
    bias_f = fetched[5].astype(jnp.float32)
    summed_in, normed_one, queries = (record[0], record[1], record[2])
    attn_out, log_tot, after_attn = (record[5], record[6], record[7])
    second_normalized, upward, gelu_output = (record[8], record[9], record[10])
    keys_all, values_all = kv_pair
    gradient_bfloat = hidden_state_gradient.astype(jnp.bfloat16)
    down_weight_gradient = jnp.einsum(
        "awt,awg->tg", gelu_output, gradient_bfloat, preferred_element_type=jnp.float32
    )
    bias_down = jnp.sum(hidden_state_gradient, axis=(0, 1))
    activation_gradient = jnp.einsum(
        "ngb,rb->ngr", gradient_bfloat, down_matrix, preferred_element_type=jnp.float32
    )
    _, gelu_back = jax.vjp(jax.nn.gelu, upward)
    grad_upward = gelu_back(activation_gradient)[0]
    bias_up = jnp.sum(grad_upward, axis=(0, 1))
    upward_bfloat = grad_upward.astype(jnp.bfloat16)
    up_weight_gradient = jnp.einsum(
        "xew,xem->wm", second_normalized, upward_bfloat, preferred_element_type=jnp.float32
    )
    second_norm_gradient = jnp.einsum(
        "iyv,tv->iyt", upward_bfloat, up_matrix, preferred_element_type=jnp.float32
    )
    _, second_back = jax.vjp(layer_norm, after_attn, gain_f[D:], bias_f[5 * D + FF :])
    from_second, gain_two, shift_two = second_back(second_norm_gradient)
    grad_mid = hidden_state_gradient + from_second
    mid_bf = grad_mid.astype(jnp.bfloat16)
    grad_out = jnp.einsum("lsc,lsd->cd", attn_out, mid_bf, preferred_element_type=jnp.float32)
    bias_out = jnp.sum(grad_mid, axis=(0, 1))
    grad_attn = jnp.einsum(
        "lsd,cd->lsc", mid_bf, mat_out, preferred_element_type=jnp.float32
    ).astype(jnp.bfloat16)
    grad_query, part_key, part_value = attend_back(
        queries, keys_all, values_all, log_tot, grad_attn
    )
    grad_key, grad_value = (
        lax.psum_scatter(
            part_key.astype(jnp.bfloat16), "seq", scatter_dimension=0, tiled=True
        ).astype(jnp.float32),
        lax.psum_scatter(
            part_value.astype(jnp.bfloat16), "seq", scatter_dimension=0, tiled=True
        ).astype(jnp.float32),
    )
    bias_query = jnp.sum(grad_query, axis=(0, 1))
    bias_value = jnp.sum(grad_value, axis=(0, 1))
    grad_linear = jnp.concatenate([grad_query, grad_key, grad_value], axis=-1).astype(jnp.bfloat16)
    grad_qkv = jnp.einsum(
        "lsc,lse->ce", normed_one, grad_linear, preferred_element_type=jnp.float32
    )
    grad_norm_one = jnp.einsum(
        "lse,ce->lsc", grad_linear, mat_qkv, preferred_element_type=jnp.float32
    )
    _, first_back = jax.vjp(layer_norm, summed_in, gain_f[:D], bias_f[4 * D + FF : 5 * D + FF])
    from_first, gain_one, shift_one = first_back(grad_norm_one)
    grad_in = grad_mid + from_first
    grad_table = jnp.dot(onehot.T, jnp.sum(grad_in, axis=0), precision=HIGH)
    grad_gain = jnp.concatenate([gain_one, gain_two])
    grad_bias = jnp.concatenate(
        [bias_query, bias_value, bias_out, bias_up, bias_down, shift_one, shift_two]
    )
    return (
        grad_in,
        (
            grad_qkv,
            grad_out,
            up_weight_gradient,
            down_weight_gradient,
            grad_gain,
            grad_bias,
            grad_table,
        ),
    )


def body(
    inputs,
    cotangent,
    w_qkv,
    w_out,
    w_up,
    w_down,
    norm_gains,
    biases,
    time_table,
    timesteps,
    importance,
):
    onehot = (timesteps[:, None] == jnp.arange(STEPS, dtype=jnp.int32)[None, :]).astype(jnp.float32)
    seq_weight = jnp.dot(onehot, importance, precision=HIGH)
    hidden = inputs.astype(jnp.float32)
    records = []
    fetched_all = []
    for layer_id in range(LAYERS):
        fetched = (
            lax.all_gather(w_qkv[layer_id], ("dp", "seq"), axis=0, tiled=True),
            lax.all_gather(w_out[layer_id], ("dp", "seq"), axis=0, tiled=True),
            lax.all_gather(w_up[layer_id], ("dp", "seq"), axis=0, tiled=True),
            lax.all_gather(w_down[layer_id], ("dp", "seq"), axis=0, tiled=True),
            lax.all_gather(norm_gains[layer_id], ("dp", "seq"), axis=0, tiled=True),
            lax.all_gather(biases[layer_id], ("dp", "seq"), axis=0, tiled=True),
            lax.all_gather(time_table[layer_id], ("dp", "seq"), axis=1, tiled=True),
        )
        hidden, record = forward_layer(hidden, fetched, onehot)
        records.append(record)
        fetched_all.append(fetched)
    hidden_state_gradient = cotangent.astype(jnp.float32) * seq_weight[None, :, None]
    shards = [None] * LAYERS
    for layer_id in reversed(range(LAYERS)):
        record = records[layer_id]
        fetched = (
            lax.all_gather(w_qkv[layer_id], ("dp", "seq"), axis=0, tiled=True),
            lax.all_gather(w_out[layer_id], ("dp", "seq"), axis=0, tiled=True),
            lax.all_gather(w_up[layer_id], ("dp", "seq"), axis=0, tiled=True),
            lax.all_gather(w_down[layer_id], ("dp", "seq"), axis=0, tiled=True),
            lax.all_gather(norm_gains[layer_id], ("dp", "seq"), axis=0, tiled=True),
            lax.all_gather(biases[layer_id], ("dp", "seq"), axis=0, tiled=True),
            lax.all_gather(time_table[layer_id], ("dp", "seq"), axis=1, tiled=True),
        )
        kv_pair = (
            lax.all_gather(record[3], "seq", axis=0, tiled=True),
            lax.all_gather(record[4], "seq", axis=0, tiled=True),
        )
        hidden_state_gradient, grads = backward_layer(
            hidden_state_gradient, fetched, record, onehot, kv_pair
        )
        shards[layer_id] = (
            lax.psum_scatter(grads[0], ("dp", "seq"), scatter_dimension=0, tiled=True),
            lax.psum_scatter(grads[1], ("dp", "seq"), scatter_dimension=0, tiled=True),
            lax.psum_scatter(grads[2], ("dp", "seq"), scatter_dimension=0, tiled=True),
            lax.psum_scatter(grads[3], ("dp", "seq"), scatter_dimension=0, tiled=True),
            lax.psum_scatter(grads[4], ("dp", "seq"), scatter_dimension=0, tiled=True),
            lax.psum_scatter(grads[5], ("dp", "seq"), scatter_dimension=0, tiled=True),
            lax.psum_scatter(grads[6], ("dp", "seq"), scatter_dimension=1, tiled=True),
        )
    stacked = [
        jnp.stack([shards[layer_id][member] for layer_id in range(LAYERS)]) for member in range(7)
    ]
    return (
        hidden,
        hidden_state_gradient,
        stacked[0],
        stacked[1],
        stacked[2],
        stacked[3],
        stacked[4],
        stacked[5],
        stacked[6],
    )


MESH_ID = pl.DeviceIdType.MESH
LOG2E = 1.4426950408889634
F32 = jnp.float32
BF = jnp.bfloat16
TILE = 256
PAIRS = HEADS // 2
N_SEMS = 256
GELU_A = math.sqrt(2.0 / math.pi)
GELU_B = 0.044715

B_Q, B_V, B_O, B_U, B_D, B_S1, B_S2 = 0, D, 2 * D, 3 * D, 3 * D + FF, 4 * D + FF, 5 * D + FF


def nn(left, right):
    return jnp.dot(left, right, preferred_element_type=F32)


def nt(left, right, precision=None):
    return lax.dot_general(left, right, (((1,), (1,)), ((), ())), preferred_element_type=F32, precision=precision)


def tn(left, right):
    return lax.dot_general(left, right, (((0,), (0,)), ((), ())), preferred_element_type=F32)


def rows_sum(value):
    return jnp.sum(value, axis=0, keepdims=True)


def ln_parts(value):
    centered = value - jnp.mean(value, axis=-1, keepdims=True)
    scale = lax.rsqrt(jnp.mean(centered * centered, axis=-1, keepdims=True) + EPS)
    return centered * scale, scale


def gelu_parts(up):
    square = up * up
    tanh = jnp.tanh(GELU_A * up * (1.0 + GELU_B * square))
    return square, tanh


class Fused:
    def __init__(self, n_z, refs):
        (self.ts, self.imp, self.xin, self.cot, self.wq_i, self.wo_i, self.wu_i, self.wd_i, self.gains_i, self.biases_i, self.tab,
         self.act_o, self.gin_o, self.gq_o, self.go_o, self.gu_o, self.gd_o, self.gg_o, self.gb_o, self.gt_o,
         self.Wq, self.Wo, self.Wu, self.Wd, self.SM, self.TS, self.TT, self.T24, self.TR, self.BV, self.GV, self.BG, self.GG,
         self.TG, self.X, self.N, self.NT, self.Q, self.KV, self.AO, self.LSE, self.DL, self.Y, self.GB, self.DO, self.G,
         self.GN, self.GL, self.ACC, self.OWN, self.PB, self.RB1, self.RB2, self.RB3,
         self.R1, self.R2, self.R3, self.R4, self.SR, self.SX, self.SY,
         self.ssem, self.rsem, self.lsem, self.credit) = refs
        dp, seq = lax.axis_index("dp"), lax.axis_index("seq")
        self.n_z = n_z
        self.dp, self.seq = dp, seq
        self.z, self.x, self.y, self.c = dp // 2, dp % 2, seq // 2, seq % 2
        self.next_sem = 0
        self.next_local = 0
        self.mine = {"z": self.z, "x": self.x, "y": self.y, "c": self.c}
        self.other = {"x": 1 - self.x, "y": 1 - self.y, "c": 1 - self.c}
        self.around = [(self.z + hop) % n_z for hop in range(n_z)]
        n_dp = 2 * n_z
        self.far_z = {hop: (dp + hop) % n_dp // 2 for hop in range(1, n_dp)}
        self.far_x = {hop: (dp + hop) % n_dp % 2 for hop in range(1, n_dp)}
        other_x, other_y = self.z * 2 + self.other["x"], self.other["y"] * 2 + self.c
        self.device = {
            **{("z", hop): (self.around[hop] * 2 + self.x, seq) for hop in range(1, n_z)},
            ("x", 1): (other_x, seq),
            ("y", 1): (dp, other_y),
            ("c", 1): (dp, self.y * 2 + self.other["c"]),
            ("p", 1): (other_x, seq),
            ("p", 2): (dp, other_y),
            ("p", 3): (other_x, other_y),
            **{("d", hop): ((dp + hop) % n_dp, seq) for hop in range(1, n_dp)},
            **{("s", hop): (dp, (seq + hop) % 4) for hop in range(1, 4)},
        }
        self.device = {key: {"dp": there[0], "seq": there[1]} for key, there in self.device.items()}

    def hops(self, dim):
        return [hop for name, hop in self.device if name == dim]

    def enter(self):
        barrier = pltpu.get_barrier_semaphore()
        who = [key for key in self.device if key[0] in "ds"] + [("p", 3)]
        for key in who:
            pl.semaphore_signal(barrier, inc=1, device_id=self.device[key], device_id_type=MESH_ID)
        pl.semaphore_wait(barrier, len(who))

    def remote(self, src, dst, dim, hop=1, number=None):
        if number is None:
            number = self.next_sem
            self.next_sem += 1
        return pltpu.make_async_remote_copy(
            src, dst, self.ssem.at[number], self.rsem.at[number], device_id=self.device[dim, hop], device_id_type=MESH_ID
        )

    def local(self, src, dst):
        number = self.next_local
        self.next_local += 1
        return pltpu.make_async_copy(src, dst, self.lsem.at[number])


class Gather:
    def __init__(self, me, view, order):
        self.copies = []
        done = ""
        for dim in order:
            block = view(*[slice(None) if other in done else me.mine[other] for other in "zxyc"])
            self.copies.append([me.remote(block, block, dim, hop) for hop in me.hops(dim)])
            done += "xy" if dim == "p" else dim

    def start(self, stage):
        if stage:
            self.arrive(stage - 1)
        for copy in self.copies[stage]:
            copy.start()

    def arrive(self, stage=-1):
        for copy in self.copies[stage]:
            copy.wait_recv()

    def drain(self):
        for copies in self.copies:
            for copy in copies:
                copy.wait_send()


class Single:
    def __init__(self, copy):
        self.copy = copy

    def start(self, stage):
        self.copy.start()


class Reduce:
    def __init__(self, me, layer, grad, recv, out, cols, order, number, before):
        self.me, self.layer, self.grad, self.recv, self.out, self.cols, self.order = me, layer, grad, recv, out, cols, order
        self.number, self.before = number, before
        self.first_sem = before.first_sem if before else me.next_sem
        self.last = len(order) - 1
        self.copies = [self.build(stage) for stage in range(len(order))]

    def block(self, fixed):
        return tuple(fixed.get(dim, slice(None)) for dim in "zxyc")

    def kept(self, stage):
        done = "".join("xy" if dim == "p" else dim for dim in self.order[:stage])
        return {dim: self.me.mine[dim] for dim in done}

    def build(self, stage):
        me, dim = self.me, self.order[stage]
        copies = []
        number = self.first_sem + sum(len(me.hops(before)) for before in self.order[:stage])
        for hop in me.hops(dim):
            fixed = self.kept(stage)
            if dim == "z":
                fixed["z"] = me.around[hop]
            elif dim == "p":
                fixed["x"] = me.mine["x"] if hop == 2 else me.other["x"]
                fixed["y"] = me.mine["y"] if hop == 1 else me.other["y"]
            else:
                fixed[dim] = me.other[dim]
            src = self.grad.at[(self.layer, *self.block(fixed), slice(None), self.cols)]
            dst = self.landed(stage, hop).at[(*self.landing(stage, hop), slice(None), self.cols)]
            copies.append(me.remote(src, dst, dim, hop, number + len(copies) if self.before else None))
        return copies

    def landed(self, stage, hop):
        return self.recv[3] if stage == self.last else self.recv[stage]

    def landing(self, stage, hop):
        dim = self.order[stage]
        if stage == self.last:
            return (hop - 1,)
        if dim == "p":
            return (slice(None), hop - 1)
        if dim == "z":
            return (slice(2 * hop - 2, 2 * hop),)
        return ((slice(0, self.me.n_z), slice(None), slice(None)), (slice(None), slice(0, 2)), (slice(0, self.me.n_z),))[stage]

    def start(self, stage):
        me = self.me
        if stage:
            self.add(stage - 1)
            dim = self.order[stage - 1]
            if self.layer == LAYERS - 1:
                for hop in me.hops(dim):
                    pl.semaphore_signal(
                        me.credit.at[self.number, stage - 1], inc=1, device_id=me.device[dim, hop], device_id_type=MESH_ID
                    )
        if stage <= self.last:
            if self.layer < LAYERS - 1:
                pl.semaphore_wait(me.credit.at[self.number, stage], len(me.hops(self.order[stage])))
                for copy in self.before.copies[stage]:
                    copy.wait_send()
            for copy in self.copies[stage]:
                copy.start()

    def add(self, stage):
        me, dim = self.me, self.order[stage]
        for copy in self.copies[stage]:
            copy.wait_recv()
        fixed = self.kept(stage + 1)
        if stage == self.last or dim in "zp":
            where = (self.layer, *self.block(fixed), slice(None), self.cols)
            total = self.grad[where].astype(F32)
            for hop in me.hops(dim):
                total = total + self.landed(stage, hop)[(*self.landing(stage, hop), slice(None), self.cols)].astype(F32)
            if stage == self.last:
                self.out[self.layer, :, self.cols] = total
            else:
                self.grad[where] = total.astype(BF)
            return

        def one(z, carry):
            where = (self.layer, *self.block({**fixed, "z": z}), slice(None), self.cols)
            came = (z, *self.landing(stage, 1)[1:], slice(None), self.cols)
            self.grad[where] = self.grad[where] + self.recv[stage][came]
            return carry

        lax.fori_loop(0, me.n_z, one, 0)

    def drain(self):
        for copies in self.copies:
            for copy in copies:
                copy.wait_send()


def at_step(index, hooks):
    for when, action in hooks:
        pl.when(index == when)(action)


BACKWARD_AT = (21, 0)
END_AT = 42
GATHER = (
    ("pzc", 0, 2, 6),
    ("yzxc", 0, 2, 5, 6),
    ("zpc", 0, 2, 3),
    ("zpc", 0, 1, 5),
    ("pzc", 0, 3, 13),
    ("pzc", 2, 3, 10),
    ("zpc", 1, 3, 6),
    ("zpc", 0, 2, 13),
    ("pzc", 0, 4, 14),
    ("zyxc", 0, 4, 11, 14),
    ("zpc", 1, 5, 15),
    ("zpc", 2, 5, 12),
    ("zpc", 7, 18, 26),
    ("zpc", 3, 8, 20),
    ("pzc", 2, 18, 29),
    ("zpc", 7, 16, 27),
    ("pzc", 0, 11, 27),
    ("zpc", 10, 18, 27),
    ("pzc", 0, 1, 2),
    ("y", 0),
    ("y", 29),
)
REDUCE = (
    ("cpz", 5, 6, 12, 28),
    ("cxzy", 4, 11, 14, 33, 38),
    ("cpz", 3, 4, 14, 25),
    ("cxzy", 11, 14, 27, 34, 41),
    ("cpz", 10, 15, 22, 32),
    ("cpz", 9, 12, 32, 35),
    ("cpz", 15, 15, 25, 36),
    ("cpz", 15, 15, 28, 39),
    ("cpz", 19, 24, 32, 35),
    ("cpz", 19, 22, 27, 35),
    ("cpz", 26, 27, 33, 37),
    ("cxzy", 25, 29, 34, 44, 46),
    ("cpz", 23, 25, 32, 43),
    ("cxzy", 32, 33, 36, 44, 46),
    ("cpz", 35, 36, 41, 43),
    ("cpz", 32, 35, 40, 44),
    ("cpz", 36, 36, 43, 46),
    ("cpz", 36, 38, 42, 44),
    ("cpz", 38, 38, 42, 44),
    ("cpz", 38, 39, 42, 44),
    ("y", 39),
)

SMALL = "small"


def pieces(name, layer):
    return 4 if name == "q" and layer == 0 else 2


def by_place(moves, plan):
    timeline = {}
    for move, (_, *places) in zip(moves, plan, strict=True):
        for stage, place in enumerate(places):
            timeline.setdefault(place, []).append((move, stage))
    return timeline


def fused_kernel(n_z, *refs):
    me = Fused(n_z, refs)
    x, y, z, c = me.x, me.y, me.z, me.c
    n_dp = 2 * n_z
    spare = slice(None)

    mats = ((me.wq_i, me.Wq), (me.wo_i, me.Wo), (me.wu_i, me.Wu), (me.wd_i, me.Wd))
    loads = [me.local(src.at[layer], dst.at[layer, z, x, y, c]) for layer in range(LAYERS) for src, dst in mats]
    for load in loads:
        load.start()
    own_tokens = [
        me.local(src.at[seq], dst.at[tile]) for src, dst in ((me.xin, me.DO), (me.cot, me.GB)) for seq, tile in ((y, 0), (2, 2))
    ]
    for load in own_tokens:
        load.start()

    row = lax.broadcasted_iota(jnp.int32, (32, 128), 0)
    steps = jnp.zeros((32, 128), jnp.int32)
    for j in range(3):
        steps = jnp.where(row == 3 * me.dp + j, me.ts[j], steps)
    me.TT[z, x] = steps

    def choose(rows, cols, first):
        here = lax.broadcasted_iota(jnp.int32, (rows, cols), 1) == first + lax.broadcasted_iota(jnp.int32, (rows, cols), 0)
        return here.astype(F32)

    own_biases, own_gains = choose(160, 640, 160 * me.seq), choose(32, 128, 32 * me.seq)
    own_lanes = choose(16, 128, 16 * (4 * x + me.seq))
    spread_b = nn(me.biases_i[...].astype(F32), own_biases)
    spread_g = nn(me.gains_i[...].astype(F32), own_gains)
    rows = []
    for layer in range(LAYERS):
        rows += [spread_b[layer : layer + 1, 128 * r : 128 * r + 128] for r in range(5)] + [spread_g[layer : layer + 1]]
    me.SM[z, x, y, c] = jnp.concatenate(rows + [jnp.zeros((16 - 6 * LAYERS, 128), F32)], axis=0).astype(BF)
    me.BG[...] = jnp.zeros_like(me.BG)
    me.GG[...] = jnp.zeros_like(me.GG)

    me.enter()
    for load in loads:
        load.wait()

    def weight(layer, ref, order, cols):
        return Gather(me, lambda *where: ref.at[(layer, *where, spare, cols)], order)

    grads = {"q": me.Wq, "o": me.Wo, "u": me.Wu, "d": me.Wd}

    steps_all = Gather(me, lambda gz, gx, gy, gc: me.TT.at[gz, gx], "d")
    times = Gather(me, lambda *where: me.TS.at[where], "zpc")
    token_in = me.remote(me.xin.at[me.other["y"]], me.DO.at[1], "y")
    cot_in = me.remote(me.cot.at[me.other["y"]], me.GB.at[1], "y")
    moves = {}
    plan = iter(GATHER)
    for layer in range(LAYERS):
        for name, ref in grads.items():
            width = ref.shape[-1] // pieces(name, layer)
            for part in range(pieces(name, layer)):
                moves[name, part, layer] = weight(layer, ref, next(plan)[0], slice(width * part, width * (part + 1)))
    moves[SMALL] = small = Gather(me, lambda *where: me.SM.at[where], next(plan)[0])
    timeline = by_place([*moves.values(), Single(token_in), Single(cot_in)], GATHER)

    def have(names, layer):
        for name in names:
            for part in range(pieces(name, layer)):
                moves[name, part, layer].arrive()

    def fire(place):
        for move, stage in timeline.get(place, ()):
            move.start(stage)

    def fires(first, count):
        return [(i, functools.partial(fire, first + i)) for i in range(count) if first + i in timeline]

    steps_all.start(0)
    fire(0)
    fire(1)
    steps_all.arrive()
    t24 = jnp.sum(me.TT[...].reshape(n_dp, 32, 128), axis=0)
    me.T24[...] = t24
    hot = (t24[:, 0:1] == lax.broadcasted_iota(jnp.int32, (32, STEPS), 1)).astype(F32).astype(BF)
    picked = jnp.concatenate([nt(hot, me.tab[layer])[:24] for layer in range(LAYERS)], axis=0).astype(BF)
    me.TS[z, x, y, c] = nn(picked, own_lanes.astype(BF)).astype(BF)
    times.start(0)
    fire(2)
    times.start(1)
    fire(3)
    times.start(2)
    fire(4)
    fire(5)

    small.arrive()
    for gz in range(n_z):
        for gx in range(2):
            block = jnp.sum(me.SM[gz, gx].reshape(4, 16, 128).astype(F32), axis=0)
            dp = 2 * gz + gx
            for layer in range(LAYERS):
                for r in range(5):
                    at = (5 * dp + r) * 128
                    me.BV[layer, :, at : at + 128] = block[6 * layer + r : 6 * layer + r + 1]
                me.GV[layer, :, 128 * dp : 128 * dp + 128] = block[6 * layer + 5 : 6 * layer + 6]
    times.arrive()
    slabs = jnp.concatenate(
        [jnp.sum(me.TS[gz].reshape(8, 48, 128).astype(F32), axis=0) for gz in range(n_z)], axis=1
    ).astype(BF)
    r8 = lax.broadcasted_iota(jnp.int32, (16, 48), 0)
    c48 = lax.broadcasted_iota(jnp.int32, (16, 48), 1)
    for layer in range(LAYERS):
        base = 24 * layer + 3 * me.dp
        pick = ((r8 == 0) & (c48 == base + y)) | ((r8 == 1) & (c48 == base + 2))
        me.TR[layer] = nn(pick.astype(F32).astype(BF), slabs)[:8]

    def time_row(layer, tile):
        return me.TR[layer, 1:2, :] if tile == 2 else me.TR[layer, 0:1, :]

    def bias(layer, at, width=D):
        return me.BV[layer, :, at : at + width]

    for load in own_tokens:
        load.wait()
    token_in.wait_recv()
    for tile in range(3):
        me.X[0, tile] = me.DO[tile].astype(F32) + time_row(0, tile)

    fire(6)
    have("q", 0)

    sends = [token_in, cot_in]

    def send(src, dst, dim):
        copy = me.remote(src, dst, dim)
        sends.append(copy)
        return copy

    def qkv(layer, tile):
        hat, _ = ln_parts(me.X[layer, tile])
        normed = (hat * me.GV[layer, :, :D] + bias(layer, B_S1)).astype(BF)
        slot = 4 if tile == 2 else tile
        lin = [nn(normed, me.Wq[layer, :, :, :, :, :, D * j : D * j + D].reshape(D, D)) for j in range(3)]
        me.Q[layer, tile] = (lin[0] + bias(layer, B_Q)).astype(BF) * jnp.asarray(1.0 / math.sqrt(HEAD_DIM), BF)
        me.KV[layer, 0, slot] = lin[1].astype(BF)
        me.KV[layer, 1, slot] = (lin[2] + bias(layer, B_V)).astype(BF)

    low_lanes = lax.broadcasted_iota(jnp.int32, (TILE, 128), 1) < HEAD_DIM

    def two_heads(pair):
        zero = jnp.zeros_like(pair)
        return jnp.concatenate([jnp.where(low_lanes, pair, zero), jnp.where(low_lanes, zero, pair)], axis=0)

    def attend_two(layer, step):
        tile, base = step // 2, step // 4 * 4
        first = step % 2 * 2
        cols = [pl.ds(pl.multiple_of((first + i) * 128, 128), 128) for i in range(2)]
        queries = [two_heads(me.Q[layer, tile, :, cols[i]]) for i in range(2)]

        def block(which, part, i):
            return me.KV[layer, which, pl.ds(base + 2 * part, 2), :, cols[i]].reshape(2 * TILE, 128)

        def scores(part, i):
            return nt(block(0, part, i), queries[i])

        def highest(parts):
            tops = [jnp.max(part, axis=0, keepdims=True) for part in parts]
            return jnp.maximum(tops[0], tops[1]) * LOG2E

        def mix(score, top, part, i):
            values = jnp.concatenate([block(1, part, i).T, jnp.ones((16, 2 * TILE), BF)], axis=0)
            return nn(values, jnp.exp2(score * LOG2E - top).astype(BF))

        def finish(mixed, top, i):
            total = mixed[128:129]
            mixed = mixed[:128] * (1.0 / total)
            me.LSE[layer, tile, first + i] = top + jnp.log2(total)
            out = jnp.concatenate([mixed[:HEAD_DIM, :TILE], mixed[HEAD_DIM:, TILE:]], axis=0)
            me.AO[layer, tile, :, cols[i]] = out.T.astype(BF)

        now = [scores(0, 0), scores(1, 0)]
        top = highest(now)
        later, mixed = [], 0.0
        for part in range(2):
            later.append(scores(part, 1))
            mixed = mixed + mix(now[part], top, part, 0)
        finish(mixed, top, 0)
        top = highest(later)
        finish(mix(later[0], top, 0, 1) + mix(later[1], top, 1, 1), top, 1)

    kv = me.KV
    to_y = [[send(kv.at[layer, i, 4], kv.at[layer, i, 5], "y") for i in range(2)] for layer in range(LAYERS)]
    on_c = [[send(kv.at[layer, i, 5], kv.at[layer, i, 7], "c") for i in range(2)] for layer in range(LAYERS)]
    to_c = [
        [send(kv.at[layer, :, a], kv.at[layer, :, b], "c") for a, b in ((0, 2), (1, 3), (4, 6))] for layer in range(LAYERS)
    ]

    def project(layer, tile):
        qkv(layer, tile)
        if tile == 2:
            for copy in to_y[layer]:
                copy.start()
        to_c[layer][tile].start()

    def attention(layer, first, last, place):
        def step(index, carry):
            at_step(index - first, fires(place, last - first))
            attend_two(layer, index)
            return carry

        lax.fori_loop(first, last, step, 0)

    def rest(layer, tiles, place):
        if tiles[0] == 0:
            have("o", layer)
        fire(place)
        w_out = me.Wo[layer].reshape(D, D)
        for tile in tiles:
            after = me.X[layer, tile] + nn(me.AO[layer, tile], w_out) + bias(layer, B_O)
            me.Y[layer, tile] = after
            hat, _ = ln_parts(after)
            me.N[tile] = (hat * me.GV[layer, :, D:] + bias(layer, B_S2)).astype(BF)
            me.GN[tile] = after + bias(layer, B_D)
        if tiles[0] == 0:
            have("ud", layer)

        def ffn(half, carry):
            at_step(half, fires(place + 1, 2))
            cols = pl.ds(pl.multiple_of(half * (FF // 2), FF // 2), FF // 2)
            w_up = me.Wu[layer, :, :, :, :, :, cols].reshape(D, FF // 2)
            w_down = me.Wd[layer, pl.ds(half * (n_z // 2), n_z // 2)].reshape(FF // 2, D)
            b_up = me.BV[layer, :, pl.ds(pl.multiple_of(B_U + half * (FF // 2), D), FF // 2)]
            for tile in tiles:
                up = nn(me.N[tile], w_up) + b_up
                _, tanh = gelu_parts(up)
                me.GN[tile] += nn((0.5 * up * (1.0 + tanh)).astype(BF), w_down)
            return carry

        lax.fori_loop(0, 2, ffn, 0)

    def pass_on(layer, i):
        to_y[layer][i].wait_recv()
        on_c[layer][i].start()

    def third_keys(layer):
        pass_on(layer, 1)
        for copy in [to_c[layer][2], *on_c[layer]]:
            copy.wait_recv()

    project(0, 2)
    fire(7)
    project(0, 0)
    fire(8)
    project(0, 1)
    fire(9)
    to_c[0][0].wait_recv()
    to_c[0][1].wait_recv()
    attention(0, 0, 4, 10)
    rest(0, (0, 1), 14)
    pass_on(0, 0)
    for tile in range(2):
        me.X[1, tile] = me.GN[tile] + time_row(1, tile)
    fire(17)
    have("q", 1)
    project(1, 0)
    project(1, 1)
    fire(18)
    third_keys(0)
    attention(0, 4, 6, 19)
    rest(0, (2,), 21)
    me.X[1, 2] = me.GN[2] + time_row(1, 2)
    project(1, 2)
    fire(24)
    to_c[1][0].wait_recv()
    to_c[1][1].wait_recv()
    attention(1, 0, 4, 25)
    rest(1, (0, 1), 29)
    pass_on(1, 0)
    act_out = [
        me.local(me.DO.at[0], me.act_o.at[y]), me.remote(me.DO.at[1], me.act_o.at[y], "y"), me.local(me.DO.at[2], me.act_o.at[2])
    ]
    for tile in range(2):
        me.DO[tile] = me.GN[tile].astype(BF)
    third_keys(1)
    attention(1, 4, 6, 32)
    rest(1, (2,), 34)
    me.DO[2] = me.GN[2].astype(BF)
    for copy in act_out:
        copy.start()

    cot_in.wait_recv()
    weight_y, weight_2 = me.imp[me.ts[y]], me.imp[me.ts[2]]
    for tile in range(3):
        grad = me.GB[tile].astype(F32) * (weight_2 if tile == 2 else weight_y)
        me.G[tile] = grad
    for part in [steps_all, times, *moves.values()]:
        part.drain()
    for copy in sends:
        copy.wait_send()
    sends.clear()

    outs = {"q": me.gq_o, "o": me.go_o, "u": me.gu_o, "d": me.gd_o}
    recvs = {
        name: [me.R1[i], me.R2[i], me.R3[i], me.R4[i]] for i, name in enumerate("qoud")
    }

    spans = {
        "d": ("d", 0, D), "u": ("u", 0, FF), "o": ("o", 0, D), "p": ("q", 0, D), "q": ("q", D, 3 * D)
    }

    plan = iter(REDUCE)

    def piece(layer, number, name, half):
        kind, begin, end = spans[name]
        width = (end - begin) // 2
        start = begin + width * half
        before = sums[number] if layer < LAYERS - 1 else None
        cols = slice(start, start + width)
        return Reduce(me, layer, grads[kind], recvs[kind], outs[kind], cols, next(plan)[0], number, before)

    def add_bias(layer, at, value):
        me.BG[layer, :, at : at + value.shape[-1]] += value

    def ln_back(layer, gain_at, shift_at, source, grad):
        hat, scale = ln_parts(source)
        me.GG[layer, :, gain_at : gain_at + D] += rows_sum(grad * hat)
        add_bias(layer, shift_at, rows_sum(grad))
        inner = grad * me.GV[layer, :, gain_at : gain_at + D]
        return scale * (inner - jnp.mean(inner, axis=-1, keepdims=True) - hat * jnp.mean(inner * hat, axis=-1, keepdims=True))

    def normed_t(layer, source, gain_at, shift_at):
        for tile in range(3):
            hat, _ = ln_parts(source[layer, tile])
            normed = (hat * me.GV[layer, :, gain_at : gain_at + D] + bias(layer, shift_at)).astype(BF)
            me.N[tile] = normed
            me.NT[:, TILE * tile : TILE * tile + TILE] = normed.T

    head_of = lax.broadcasted_iota(jnp.int32, (HEADS, D), 1) // HEAD_DIM
    selector = (head_of == lax.broadcasted_iota(jnp.int32, (HEADS, D), 0)).astype(F32)

    def backward(layer, before_out, tail):
        base = BACKWARD_AT[layer]
        normed_t(layer, me.Y, D, B_S2)
        for tile in range(3):
            me.GB[tile] = me.G[tile].astype(BF)
            add_bias(layer, B_D, rows_sum(me.G[tile]))
            me.GN[tile] = jnp.zeros((TILE, D), F32)

        def ffn(slab, carry):
            at_step(slab, fires(base, n_z))
            cols = pl.ds(pl.multiple_of(slab * D, D), D)
            b_cols = pl.ds(pl.multiple_of(B_U + slab * D, D), D)
            w_up = me.Wu[layer, :, :, :, :, :, cols].reshape(D, D)
            w_down = me.Wd[layer, slab].reshape(D, D)
            grads_h = me.GB[...].reshape(3 * TILE, D)
            up = nn(me.N[...].reshape(3 * TILE, D), w_up) + me.BV[layer, :, b_cols]
            square, tanh = gelu_parts(up)
            active = (0.5 * up * (1.0 + tanh)).astype(BF)
            slope = 0.5 * (1.0 + tanh) + (0.5 * GELU_A) * up * (1.0 - tanh * tanh) * (1.0 + 3.0 * GELU_B * square)
            grad_up = nt(grads_h, w_down) * slope
            me.BG[layer, :, b_cols] += rows_sum(grad_up)
            grad_up = grad_up.astype(BF)
            me.GN[...] += nt(grad_up, w_up).reshape(3, TILE, D)
            me.Wd[layer, slab] = tn(active, grads_h).astype(BF).reshape(2, 2, 2, 64, D)
            me.Wu[layer, :, :, :, :, :, cols] = nn(me.NT[...], grad_up).astype(BF).reshape(n_z, 2, 2, 2, 16, D)
            return carry

        lax.fori_loop(0, n_z, ffn, 0)
        fire(base + 4)
        for tile in range(3):
            mid = me.G[tile] + ln_back(layer, D, B_S2, me.Y[layer, tile], me.GN[tile])
            me.G[tile] = mid
            add_bias(layer, B_O, rows_sum(mid))
            me.GB[tile] = mid.astype(BF)
        fire(base + 5)
        before_out()
        w_out = me.Wo[layer].reshape(D, D)
        for tile in range(3):
            grad_attn = nt(me.GB[tile], w_out).astype(BF)
            me.DO[tile] = grad_attn
            delta = nt(selector, grad_attn.astype(F32) * me.AO[layer, tile].astype(F32), lax.Precision.HIGHEST)
            for pair in range(PAIRS):
                both = jnp.concatenate([delta[2 * pair : 2 * pair + 1], delta[2 * pair + 1 : 2 * pair + 2]], axis=1)
                me.DL[tile, pair] = both
        d_out = tn(me.AO[layer].reshape(3 * TILE, D), me.GB[...].reshape(3 * TILE, D))
        me.Wo[layer] = d_out.astype(BF).reshape(n_z, 2, 2, 2, 16, D)
        fire(base + 6)

        me.ACC[...] = jnp.zeros_like(me.ACC)
        third_c = send(me.PB.at[:, 1:3], me.RB1, "c")
        third_y = send(me.PB.at[:, 0], me.RB2, "y")
        from_c = me.remote(me.GL.at[0:2, :, D:], me.RB3, "c")

        def third_done():
            me.OWN[...] = me.ACC[:, 0:TILE]
            me.PB[...] = me.ACC[:, TILE : 4 * TILE].reshape(2, 3, TILE, D).astype(BF)
            me.ACC[...] = jnp.zeros_like(me.ACC)
            third_c.start()

        def third_on():
            third_c.wait_recv()
            me.OWN[...] += me.RB1[:, 0].astype(F32)
            me.PB[:, 0] = me.PB[:, 0] + me.RB1[:, 1]
            third_y.start()

        def attend_back(step, carry):
            at_step(step, [(2, third_done), (3, third_on)] + fires(base + 8, 6))
            tile = (step // 2 + 2) % 3
            slot = tile // 2 * 4
            for i in range(2):
                pair = step % 2 * 2 + i
                cols = pl.ds(pl.multiple_of(pair * 128, 128), 128)
                queries, grads_o = two_heads(me.Q[layer, tile, :, cols]), two_heads(me.DO[tile, :, cols])
                log_sum, delta = me.LSE[layer, tile, pair], me.DL[tile, pair]
                d_query = jnp.zeros((128, 2 * TILE), F32)
                for part in range(4):
                    keys, values = me.KV[layer, 0, slot + part, :, cols], me.KV[layer, 1, slot + part, :, cols]
                    rows = slice(TILE * part, TILE * part + TILE)
                    prob = jnp.exp2(nt(keys, queries) * LOG2E - log_sum)
                    grad_s = (prob * (nt(values, grads_o) - delta)).astype(BF)
                    me.ACC[1, rows, cols] += nn(prob.astype(BF), grads_o)
                    me.ACC[0, rows, cols] += nn(grad_s, queries)
                    d_query = d_query + nn(keys.T, grad_s)
                d_query = jnp.concatenate([d_query[:HEAD_DIM, :TILE], d_query[HEAD_DIM:, TILE:]], axis=0).T
                d_query = d_query * (1.0 / math.sqrt(HEAD_DIM))
                me.BG[layer, :, cols] += rows_sum(d_query)
                me.GL[tile, :, cols] = d_query.astype(BF)
            return carry

        fire(base + 7)
        lax.fori_loop(0, 6, attend_back, 0)
        for tile in range(2):
            for i in range(2):
                rows = slice(TILE * (2 + tile), TILE * (3 + tile))
                me.GL[tile, :, D * (1 + i) : D * (2 + i)] = me.ACC[i, rows].astype(BF)
        from_c.start()
        normed_t(layer, me.X, 0, B_S1)
        fire(base + 14)

        def qkv_back(first, last):
            w_qkv = me.Wq[layer, :, :, :, :, :, first:last].reshape(D, last - first)
            for tile in range(3):
                part = nt(me.GL[tile, :, first:last], w_qkv)
                me.GN[tile] = part if first == 0 else me.GN[tile] + part
            for j in range(first, last, D):
                d_qkv = nn(me.NT[...], me.GL[:, :, j : j + D].reshape(3 * TILE, D))
                me.Wq[layer, :, :, :, :, :, j : j + D] = d_qkv.astype(BF).reshape(n_z, 2, 2, 2, 16, D)

        qkv_back(0, D)
        fire(base + 15)
        from_c.wait()
        for tile in range(2):
            rows = slice(TILE * tile, TILE * tile + TILE)
            key = me.ACC[0, rows] + me.RB3[tile, :, :D].astype(F32)
            value = me.ACC[1, rows] + me.RB3[tile, :, D:].astype(F32)
            add_bias(layer, B_V, rows_sum(value))
            me.GL[tile, :, D : 2 * D] = key.astype(BF)
            me.GL[tile, :, 2 * D :] = value.astype(BF)
        third_y.wait_recv()
        third = me.OWN[...] + me.RB2[...].astype(F32)
        me.GL[2, :, D : 2 * D] = third[0].astype(BF)
        me.GL[2, :, 2 * D :] = third[1].astype(BF)
        add_bias(layer, B_V, rows_sum(third[1]))
        fire(base + 16)
        qkv_back(D, 3 * D)
        fire(base + 17)
        totals = []
        for tile in (1, 0, 2):
            grad = me.G[tile] + ln_back(layer, 0, B_S1, me.X[layer, tile], me.GN[tile])
            me.G[tile] = grad
            totals.append(rows_sum(grad))
            tail(tile, grad)
            fire(base + 17 + len(totals))
        me.TG[layer, 0:1] = totals[0] + totals[1]
        me.TG[layer, 1:2] = totals[2]
        for copy in sends:
            copy.wait_send()
        sends.clear()

    sums = []
    for layer in reversed(range(LAYERS)):
        for number, (name, half) in enumerate((name, half) for name in spans for half in range(2)):
            sums.append(piece(layer, number, name, half))
    timeline.clear()
    gin_out = me.remote(me.GB.at[1], me.gin_o.at[y], "y")
    timeline.update(by_place([*sums, Single(gin_out)], REDUCE))

    def act_done():
        for copy in act_out:
            copy.wait()

    backward(1, act_done, lambda tile, grad: None)
    finals = []

    def out_tile(tile, grad):
        me.GB[tile] = grad.astype(BF)
        if tile != 1:
            finals.append(me.local(me.GB.at[tile], me.gin_o.at[y if tile == 0 else 2]))
            finals[-1].start()

    backward(0, lambda: None, out_tile)

    for gz in range(n_z):
        lanes = slice(128 * gz, 128 * gz + 128)
        for gx in range(2):
            dp = 2 * gz + gx
            for layer in range(LAYERS):
                for r in range(5):
                    at_lane = (5 * dp + r) * 128
                    me.SR[gz, gx, 6 * layer + r : 6 * layer + r + 1] = me.BG[layer, :, at_lane : at_lane + 128]
                me.SR[gz, gx, 6 * layer + 5 : 6 * layer + 6] = me.GG[layer, :, 128 * dp : 128 * dp + 128]
                me.SR[gz, gx, 12 + 2 * layer : 14 + 2 * layer] = me.TG[layer, 0:2, lanes]
    to_dp = [
        me.remote(me.SR.at[me.far_z[hop], me.far_x[hop]], me.SX.at[me.dp], "d", hop) for hop in me.hops("d")
    ]
    for copy in to_dp:
        copy.start()
    me.SX[me.dp] = me.SR[z, x]
    fire(END_AT)
    for copy in to_dp:
        copy.wait_recv()
    fire(END_AT + 1)
    me.SY[0, 0:16] = jnp.sum(me.SX[...], axis=0)
    for dp in range(n_dp):
        for layer in range(LAYERS):
            at_row = 16 + 24 * layer + 3 * dp
            first_seq = me.SX[dp, 12 + 2 * layer : 13 + 2 * layer]
            me.SY[0, at_row : at_row + 1] = jnp.where(y == 0, first_seq, 0.0)
            me.SY[0, at_row + 1 : at_row + 2] = jnp.where(y == 1, first_seq, 0.0)
            me.SY[0, at_row + 2 : at_row + 3] = me.SX[dp, 13 + 2 * layer : 14 + 2 * layer]
    to_seq = [me.remote(me.SY.at[0], me.SY.at[hop], "s", hop) for hop in me.hops("s")]
    for copy in to_seq:
        copy.start()
    fire(END_AT + 2)
    for copy in to_seq:
        copy.wait_recv()
    fire(END_AT + 3)
    total = me.SY[0] + me.SY[1] + me.SY[2] + me.SY[3]
    hot = (me.T24[0:24, 0:1] == lax.broadcasted_iota(jnp.int32, (24, STEPS), 1)).astype(F32)
    for layer in range(LAYERS):
        bias_row = jnp.concatenate([total[6 * layer + r : 6 * layer + r + 1] for r in range(5)], axis=1)
        me.gb_o[layer : layer + 1] = nt(bias_row, own_biases, HIGH)
        me.gg_o[layer : layer + 1] = nt(total[6 * layer + 5 : 6 * layer + 6], own_gains, HIGH)
        by_seq = nt(own_lanes, total[16 + 24 * layer : 40 + 24 * layer], HIGH)
        me.gt_o[layer] = jnp.dot(by_seq, hot, precision=HIGH, preferred_element_type=F32)
    fire(END_AT + 4)

    for copy in to_dp + to_seq:
        copy.wait_send()
    for copy in [gin_out, *finals]:
        copy.wait()
    for part in sums[len(sums) // 2 :]:
        part.drain()


def fused_call(n_z, *operands):
    any_space, vmem, smem = (pl.BlockSpec(memory_space=space) for space in (pl.ANY, pltpu.VMEM, pltpu.SMEM))
    cube = (n_z, 2, 2, 2)
    tokens = (3, TILE, D)
    sizes = ((16, 3 * D), (16, D), (16, FF), (64, D))

    def many(lead):
        return [tuple(pltpu.VMEM((*lead, *size), BF) for size in sizes)]

    flat, tree = jax.tree.flatten(
        [pltpu.VMEM((LAYERS, *cube, *size), BF) for size in sizes]
        + [
            pltpu.VMEM((*cube, 16, 128), BF),
            pltpu.VMEM((*cube, 48, 128), BF),
            pltpu.VMEM((n_z, 2, 32, 128), jnp.int32),
            pltpu.VMEM((32, 128), jnp.int32),
            pltpu.VMEM((LAYERS, 8, D), F32),
            pltpu.VMEM((LAYERS, 1, 6 * D + FF), F32),
            pltpu.VMEM((LAYERS, 1, 2 * D), F32),
            pltpu.VMEM((LAYERS, 1, 6 * D + FF), F32),
            pltpu.VMEM((LAYERS, 1, 2 * D), F32),
            pltpu.VMEM((LAYERS, 8, D), F32),
            pltpu.VMEM((LAYERS, *tokens), F32),
            pltpu.VMEM(tokens, BF),
            pltpu.VMEM((D, 3 * TILE), BF),
            pltpu.VMEM((LAYERS, *tokens), BF),
            pltpu.VMEM((LAYERS, 2, 8, TILE, D), BF),
            pltpu.VMEM((LAYERS, *tokens), BF),
            pltpu.VMEM((LAYERS, 3, PAIRS, 1, 2 * TILE), F32),
            pltpu.VMEM((3, PAIRS, 1, 2 * TILE), F32),
            pltpu.VMEM((LAYERS, *tokens), F32),
            pltpu.VMEM(tokens, BF),
            pltpu.VMEM(tokens, BF),
            pltpu.VMEM(tokens, F32),
            pltpu.VMEM(tokens, F32),
            pltpu.VMEM((3, TILE, 3 * D), BF),
            pltpu.VMEM((2, 4 * TILE, D), F32),
            pltpu.VMEM((2, TILE, D), F32),
            pltpu.VMEM((2, 3, TILE, D), BF),
            pltpu.VMEM((2, 2, TILE, D), BF),
            pltpu.VMEM((2, TILE, D), BF),
            pltpu.VMEM((2, TILE, 2 * D), BF),
        ]
        + many((n_z, 2, 2))
        + many((n_z, 3))
        + many((2 * n_z - 2,))
        + many((n_z - 1,))
        + [
            pltpu.VMEM((n_z, 2, 16, 128), F32),
            pltpu.VMEM((2 * n_z, 16, 128), F32),
            pltpu.VMEM((4, 64, 128), F32),
            pltpu.SemaphoreType.DMA((N_SEMS,)),
            pltpu.SemaphoreType.DMA((N_SEMS,)),
            pltpu.SemaphoreType.DMA((32,)),
            pltpu.SemaphoreType.REGULAR((10, 4)),
        ]
    )
    outs = [
        jax.ShapeDtypeStruct(tokens, BF),
        jax.ShapeDtypeStruct(tokens, BF),
        *[jax.ShapeDtypeStruct((LAYERS, *size), F32) for size in sizes],
        jax.ShapeDtypeStruct((LAYERS, 32), F32),
        jax.ShapeDtypeStruct((LAYERS, 160), F32),
        jax.ShapeDtypeStruct((LAYERS, 16, STEPS), F32),
    ]

    def run(*refs):
        head = len(operands) + len(outs)
        fused_kernel(n_z, *refs[:head], *jax.tree.unflatten(tree, refs[head:]))

    return pl.pallas_call(
        run,
        out_shape=outs,
        in_specs=[smem, smem] + [any_space] * 6 + [vmem] * 3,
        out_specs=[any_space] * 2 + [vmem] * 7,
        scratch_shapes=flat,
        compiler_params=pltpu.CompilerParams(collective_id=0, has_side_effects=True, vmem_limit_bytes=VMEM_BYTES),
    )(*operands)


VMEM_BYTES = 127 * 512 * 1024


def fused_body(
    inputs, cotangent, w_qkv, w_out, w_up, w_down, norm_gains, biases, time_table, timesteps, importance
):
    act, grad_in, g_qkv, g_out, g_up, g_down, grad_gains, grad_biases, grad_table = fused_call(
        lax.axis_size("dp") // 2, timesteps, importance, jnp.swapaxes(inputs, 0, 1), jnp.swapaxes(cotangent, 0, 1),
        w_qkv, w_out, w_up, w_down, norm_gains, biases, jnp.swapaxes(time_table, 1, 2),
    )
    return (
        jnp.swapaxes(act, 0, 1).astype(F32), jnp.swapaxes(grad_in, 0, 1).astype(F32), g_qkv, g_out, g_up, g_down,
        grad_gains, grad_biases, jnp.swapaxes(grad_table, 1, 2),
    )


def solution(mesh):
    devices = mesh.shape["dp"] * mesh.shape["seq"]
    whole_tiles = mesh.shape["seq"] == 4 and mesh.shape["dp"] % 2 == 0 and D // devices == 16
    in_specs = (
        P("seq", "dp", None),
        P("seq", "dp", None),
        P(None, ("dp", "seq"), None),
        P(None, ("dp", "seq"), None),
        P(None, ("dp", "seq"), None),
        P(None, ("dp", "seq"), None),
        P(None, ("dp", "seq")),
        P(None, ("dp", "seq")),
        P(None, None, ("dp", "seq")),
        P("dp"),
        P(),
    )
    out_specs = (
        P("seq", "dp", None),
        P("seq", "dp", None),
        P(None, ("dp", "seq"), None),
        P(None, ("dp", "seq"), None),
        P(None, ("dp", "seq"), None),
        P(None, ("dp", "seq"), None),
        P(None, ("dp", "seq")),
        P(None, ("dp", "seq")),
        P(None, None, ("dp", "seq")),
    )
    return jax.shard_map(
        fused_body if whole_tiles else body, mesh=mesh, in_specs=in_specs, out_specs=out_specs, check_vma=False)
```

profile of v0, /device:TPU:0, one launch (start us, length us, event | category | flops | bytes accessed | tf_op | source)
XLA Modules:
  0.0 213.3 jit_solution(7582710922841210114)
XLA Ops:
  0.6 204.2 %shard_map.178 = (bf16[3,256,512]{2,1,0:T(8,128)(2,1)}, bf16[3,256,512]{2,1,0:T(8,128)(2,1)}, f32[2,16,1536]{2,1,0:T(8,128)}, f32[2,16,512]{2,1,0:T(8,128)}, f32...) custom-call(s32[3]{0:T(128)} %refs_0_.1, ...), custom_call_target="tpu_custom_call" | custom-call | tf_op jit(solution)/shard_map/pallas_call | solution.py:1272
  204.9 0.0 copy-start.2
  204.9 0.0 copy-start.4
  204.9 0.0 copy-start.1
  204.9 0.0 copy-start
  204.9 3.5 %convert_bitcast_fusion = (f32[256,3,512]{2,0,1:T(8,128)}, f32[256,3,512]{2,0,1:T(8,128)}) fusion(bf16[3,256,512]{2,1,0:T(8,128)(2,1)} %get-tuple-element.19, bf16[3,256,512]{2,1,0:T(8,128)(2,1)} %get-tuple-element.18), kind=kLoop, calls=%fused_computation | loop fusion | flops 786432 | bytes 4718592 | tf_op jit(solution)/shard_map/convert_element_type | solution.py:1293
  208.5 0.0 copy-start.6
  208.5 0.0 copy-start.5
  208.5 0.0 copy-start.3
  208.5 0.0 copy-done.2
  208.5 0.7 copy.27
  209.2 0.0 copy-done.4
  209.2 0.6 copy.28
  209.8 0.0 copy-done.1
  209.8 0.7 copy.29
  210.5 0.0 copy-done
  210.5 0.7 copy.30
  211.2 0.0 copy-done.6
  211.2 0.6 copy.31
  211.8 0.0 copy-done.5
  211.8 0.6 copy.32
  212.4 0.0 copy-done.3
  212.4 0.7 copy.33
Async XLA Ops:
  204.9 3.6 %copy-start.2 = (f32[2,16,1536]{2,1,0:T(8,128)S(1)}, f32[2,16,1536]{2,1,0:T(8,128)}, u32[]{:S(2)}) copy-start(f32[2,16,1536]{2,1,0:T(8,128)} %get-tuple-element.40) | copy-start | bytes 589828
  204.9 4.3 %copy-start.4 = (f32[2,16,512]{2,1,0:T(8,128)S(1)}, f32[2,16,512]{2,1,0:T(8,128)}, u32[]{:S(2)}) copy-start(f32[2,16,512]{2,1,0:T(8,128)} %get-tuple-element.41) | copy-start | bytes 196612
  204.9 4.9 %copy-start.1 = (f32[2,16,2048]{2,1,0:T(8,128)S(1)}, f32[2,16,2048]{2,1,0:T(8,128)}, u32[]{:S(2)}) copy-start(f32[2,16,2048]{2,1,0:T(8,128)} %get-tuple-element.42) | copy-start | bytes 786436
  204.9 5.6 %copy-start = (f32[2,64,512]{2,1,0:T(8,128)S(1)}, f32[2,64,512]{2,1,0:T(8,128)}, u32[]{:S(2)}) copy-start(f32[2,64,512]{2,1,0:T(8,128)} %get-tuple-element.43) | copy-start | bytes 786436
  208.5 2.7 %copy-start.6 = (f32[2,32]{1,0:T(2,128)S(1)}, f32[2,32]{1,0:T(2,128)}, u32[]{:S(2)}) copy-start(f32[2,32]{1,0:T(2,128)} %get-tuple-element.44) | copy-start | bytes 772
  208.5 3.3 %copy-start.5 = (f32[2,160]{1,0:T(2,128)S(1)}, f32[2,160]{1,0:T(2,128)}, u32[]{:S(2)}) copy-start(f32[2,160]{1,0:T(2,128)} %get-tuple-element.45) | copy-start | bytes 3844
  208.5 3.9 %copy-start.3 = (f32[2,16,1000]{2,1,0:T(8,128)S(1)}, f32[2,16,1000]{2,1,0:T(8,128)}, u32[]{:S(2)}) copy-start(f32[2,16,1000]{2,1,0:T(8,128)} %get-tuple-element.26) | copy-start | bytes 384004
where the time goes:
time: 217 us; the launch traced here: 213 us
  Pallas kernels  204 us (94%)
  local copies, waits for them, and re-layouts  4.54 us (2%)
  other arithmetic  3.53 us (2%)
    pallas_call x1, Pallas kernels, fused_call(): pl.pallas_call(run, out_shape=outs, in_specs=[smem, smem] + [any_space] *...  204 us
    unnamed x21, local copies, waits for them, and re-layouts  4.54 us

commit v1 on v0

--- a/solution.py
+++ b/solution.py
@@ -589,50 +589,50 @@
 BACKWARD_AT = (21, 0)
 END_AT = 42
 GATHER = (
-    ("pzc", 0, 2, 6),
-    ("yzxc", 0, 2, 5, 6),
-    ("zpc", 0, 2, 3),
-    ("zpc", 0, 1, 5),
-    ("pzc", 0, 3, 13),
-    ("pzc", 2, 3, 10),
-    ("zpc", 1, 3, 6),
-    ("zpc", 0, 2, 13),
-    ("pzc", 0, 4, 14),
-    ("zyxc", 0, 4, 11, 14),
-    ("zpc", 1, 5, 15),
-    ("zpc", 2, 5, 12),
-    ("zpc", 7, 18, 26),
-    ("zpc", 3, 8, 20),
-    ("pzc", 2, 18, 29),
-    ("zpc", 7, 16, 27),
-    ("pzc", 0, 11, 27),
-    ("zpc", 10, 18, 27),
-    ("pzc", 0, 1, 2),
+    ("yzxc", 0, 2, 3, 4),
+    ("zpc", 0, 2, 4),
+    ("zpc", 0, 3, 6),
+    ("yzxc", 0, 2, 3, 6),
+    ("pzc", 2, 4, 14),
+    ("zpc", 1, 5, 10),
+    ("zpc", 2, 7, 14),
+    ("zpc", 2, 9, 18),
+    ("zpc", 0, 3, 11),
+    ("pzc", 1, 3, 12),
+    ("zpc", 3, 16, 21),
+    ("zpc", 6, 17, 21),
+    ("zpc", 2, 20, 32),
+    ("zpc", 7, 22, 32),
+    ("yzxc", 2, 8, 21, 32),
+    ("pzc", 1, 10, 28),
+    ("pzc", 17, 22, 33),
+    ("zpc", 8, 23, 32),
+    ("zpc", 0, 2, 5),
     ("y", 0),
-    ("y", 29),
+    ("y", 23),
 )
 REDUCE = (
-    ("cpz", 5, 6, 12, 28),
-    ("cxzy", 4, 11, 14, 33, 38),
-    ("cpz", 3, 4, 14, 25),
-    ("cxzy", 11, 14, 27, 34, 41),
-    ("cpz", 10, 15, 22, 32),
-    ("cpz", 9, 12, 32, 35),
-    ("cpz", 15, 15, 25, 36),
-    ("cpz", 15, 15, 28, 39),
-    ("cpz", 19, 24, 32, 35),
-    ("cpz", 19, 22, 27, 35),
-    ("cpz", 26, 27, 33, 37),
-    ("cxzy", 25, 29, 34, 44, 46),
-    ("cpz", 23, 25, 32, 43),
-    ("cxzy", 32, 33, 36, 44, 46),
-    ("cpz", 35, 36, 41, 43),
-    ("cpz", 32, 35, 40, 44),
-    ("cpz", 36, 36, 43, 46),
-    ("cpz", 36, 38, 42, 44),
+    ("cxzy", 9, 11, 15, 28, 43),
+    ("cxyz", 9, 12, 21, 35, 41),
+    ("cpz", 2, 5, 12, 15),
+    ("cpz", 4, 7, 13, 32),
+    ("cpz", 6, 14, 24, 37),
+    ("cpz", 7, 15, 29, 34),
+    ("cpz", 15, 20, 29, 40),
+    ("cpz", 15, 15, 32, 40),
+    ("cpz", 17, 22, 33, 40),
+    ("cpz", 18, 21, 33, 36),
+    ("cxzy", 28, 30, 36, 44, 44),
+    ("cxyz", 29, 32, 36, 42, 44),
+    ("cpz", 23, 24, 33, 44),
+    ("cpz", 25, 27, 33, 43),
+    ("cpz", 27, 30, 41, 45),
+    ("cpz", 28, 30, 39, 42),
+    ("cpz", 36, 38, 42, 46),
+    ("cpz", 36, 36, 41, 42),
     ("cpz", 38, 38, 42, 44),
-    ("cpz", 38, 39, 42, 44),
-    ("y", 39),
+    ("cpz", 38, 40, 43, 46),
+    ("y", 41),
 )
 
 SMALL = "small"
@@ -768,12 +768,8 @@
 
     for load in own_tokens:
         load.wait()
-    token_in.wait_recv()
-    for tile in range(3):
+    for tile in (0, 2):
         me.X[0, tile] = me.DO[tile].astype(F32) + time_row(0, tile)
-
-    fire(6)
-    have("q", 0)
 
     sends = [token_in, cot_in]
 
@@ -782,14 +778,16 @@
         sends.append(copy)
         return copy
 
-    def qkv(layer, tile):
+    def attention_norm(layer, tile):
         hat, _ = ln_parts(me.X[layer, tile])
-        normed = (hat * me.GV[layer, :, :D] + bias(layer, B_S1)).astype(BF)
-        slot = 4 if tile == 2 else tile
-        lin = [nn(normed, me.Wq[layer, :, :, :, :, :, D * j : D * j + D].reshape(D, D)) for j in range(3)]
-        me.Q[layer, tile] = (lin[0] + bias(layer, B_Q)).astype(BF) * jnp.asarray(1.0 / math.sqrt(HEAD_DIM), BF)
-        me.KV[layer, 0, slot] = lin[1].astype(BF)
-        me.KV[layer, 1, slot] = (lin[2] + bias(layer, B_V)).astype(BF)
+        return (hat * me.GV[layer, :, :D] + bias(layer, B_S1)).astype(BF)
+
+    def columns(layer, normed, j):
+        return nn(normed, me.Wq[layer, :, :, :, :, :, D * j : D * j + D].reshape(D, D))
+
+    def keys_values(layer, normed, slot):
+        me.KV[layer, 0, slot] = columns(layer, normed, 1).astype(BF)
+        me.KV[layer, 1, slot] = (columns(layer, normed, 2) + bias(layer, B_V)).astype(BF)
 
     low_lanes = lax.broadcasted_iota(jnp.int32, (TILE, 128), 1) < HEAD_DIM
 
@@ -835,18 +833,27 @@
         finish(mix(later[0], top, 0, 1) + mix(later[1], top, 1, 1), top, 1)
 
     kv = me.KV
-    to_y = [[send(kv.at[layer, i, 4], kv.at[layer, i, 5], "y") for i in range(2)] for layer in range(LAYERS)]
-    on_c = [[send(kv.at[layer, i, 5], kv.at[layer, i, 7], "c") for i in range(2)] for layer in range(LAYERS)]
+    to_y = [me.remote(me.N.at[2], me.PB.at[0, layer], "y") for layer in range(LAYERS)]
+    on_c = [send(kv.at[layer, :, 5], kv.at[layer, :, 7], "c") for layer in range(LAYERS)]
     to_c = [
         [send(kv.at[layer, :, a], kv.at[layer, :, b], "c") for a, b in ((0, 2), (1, 3), (4, 6))] for layer in range(LAYERS)
     ]
 
+    def announce(layer):
+        me.N[2] = attention_norm(layer, 2)
+        to_y[layer].start()
+
     def project(layer, tile):
-        qkv(layer, tile)
-        if tile == 2:
-            for copy in to_y[layer]:
-                copy.start()
+        normed = me.N[2] if tile == 2 else attention_norm(layer, tile)
+        keys_values(layer, normed, 4 if tile == 2 else tile)
         to_c[layer][tile].start()
+        queries = (columns(layer, normed, 0) + bias(layer, B_Q)).astype(BF)
+        me.Q[layer, tile] = queries * jnp.asarray(1.0 / math.sqrt(HEAD_DIM), BF)
+
+    def neighbour(layer):
+        to_y[layer].wait_recv()
+        keys_values(layer, me.PB[0, layer], 5)
+        on_c[layer].start()
 
     def attention(layer, first, last, place):
         def step(index, carry):
@@ -884,53 +891,51 @@
 
         lax.fori_loop(0, 2, ffn, 0)
 
-    def pass_on(layer, i):
-        to_y[layer][i].wait_recv()
-        on_c[layer][i].start()
-
     def third_keys(layer):
-        pass_on(layer, 1)
-        for copy in [to_c[layer][2], *on_c[layer]]:
-            copy.wait_recv()
-
+        to_y[layer].wait_send()
+        to_c[layer][2].wait_recv()
+        on_c[layer].wait_recv()
+
+    announce(0)
+    fire(6)
+    have("q", 0)
     project(0, 2)
     fire(7)
     project(0, 0)
     fire(8)
+    token_in.wait_recv()
+    me.X[0, 1] = me.DO[1].astype(F32) + time_row(0, 1)
     project(0, 1)
     fire(9)
+    neighbour(0)
     to_c[0][0].wait_recv()
     to_c[0][1].wait_recv()
-    attention(0, 0, 4, 10)
-    rest(0, (0, 1), 14)
-    pass_on(0, 0)
-    for tile in range(2):
-        me.X[1, tile] = me.GN[tile] + time_row(1, tile)
-    fire(17)
-    have("q", 1)
-    project(1, 0)
-    project(1, 1)
-    fire(18)
-    third_keys(0)
-    attention(0, 4, 6, 19)
-    rest(0, (2,), 21)
-    me.X[1, 2] = me.GN[2] + time_row(1, 2)
-    project(1, 2)
-    fire(24)
-    to_c[1][0].wait_recv()
-    to_c[1][1].wait_recv()
-    attention(1, 0, 4, 25)
-    rest(1, (0, 1), 29)
-    pass_on(1, 0)
+    for layer in range(LAYERS):
+        at = (10, 25)[layer]
+        attention(layer, 0, 4, at)
+        fire(at + 4)
+        if layer:
+            neighbour(layer)
+        fire(at + 5)
+        third_keys(layer)
+        attention(layer, 4, 6, at + 6)
+        rest(layer, (0, 1, 2), at + 8)
+        if layer == 0:
+            for tile in range(3):
+                me.X[1, tile] = me.GN[tile] + time_row(1, tile)
+            announce(1)
+            fire(21)
+            have("q", 1)
+            for turn, tile in enumerate((2, 0, 1)):
+                project(1, tile)
+                fire(22 + turn)
+            to_c[1][0].wait_recv()
+            to_c[1][1].wait_recv()
     act_out = [
         me.local(me.DO.at[0], me.act_o.at[y]), me.remote(me.DO.at[1], me.act_o.at[y], "y"), me.local(me.DO.at[2], me.act_o.at[2])
     ]
-    for tile in range(2):
+    for tile in range(3):
         me.DO[tile] = me.GN[tile].astype(BF)
-    third_keys(1)
-    attention(1, 4, 6, 32)
-    rest(1, (2,), 34)
-    me.DO[2] = me.GN[2].astype(BF)
     for copy in act_out:
         copy.start()
 
@@ -1033,20 +1038,24 @@
         fire(base + 6)
 
         me.ACC[...] = jnp.zeros_like(me.ACC)
-        third_c = send(me.PB.at[:, 1:3], me.RB1, "c")
-        third_y = send(me.PB.at[:, 0], me.RB2, "y")
+        third_c = send(me.PB, me.RB1, "c")
+        third_y = me.remote(me.GL.at[2, :, D:], me.RB2, "y")
         from_c = me.remote(me.GL.at[0:2, :, D:], me.RB3, "c")
 
         def third_done():
             me.OWN[...] = me.ACC[:, 0:TILE]
-            me.PB[...] = me.ACC[:, TILE : 4 * TILE].reshape(2, 3, TILE, D).astype(BF)
+            for i in range(2):
+                me.GL[2, :, D * (1 + i) : D * (2 + i)] = me.ACC[i, TILE : 2 * TILE].astype(BF)
+            me.PB[...] = me.ACC[:, 2 * TILE :].reshape(2, 2, TILE, D).astype(BF)
             me.ACC[...] = jnp.zeros_like(me.ACC)
             third_c.start()
 
         def third_on():
             third_c.wait_recv()
             me.OWN[...] += me.RB1[:, 0].astype(F32)
-            me.PB[:, 0] = me.PB[:, 0] + me.RB1[:, 1]
+            for i in range(2):
+                cols = slice(D * (1 + i), D * (2 + i))
+                me.GL[2, :, cols] = me.GL[2, :, cols] + me.RB1[i, 1]
             third_y.start()
 
         def attend_back(step, carry):
@@ -1085,9 +1094,8 @@
 
         def qkv_back(first, last):
             w_qkv = me.Wq[layer, :, :, :, :, :, first:last].reshape(D, last - first)
-            for tile in range(3):
-                part = nt(me.GL[tile, :, first:last], w_qkv)
-                me.GN[tile] = part if first == 0 else me.GN[tile] + part
+            part = nt(me.GL[:, :, first:last].reshape(3 * TILE, last - first), w_qkv).reshape(3, TILE, D)
+            me.GN[...] = part if first == 0 else me.GN[...] + part
             for j in range(first, last, D):
                 d_qkv = nn(me.NT[...], me.GL[:, :, j : j + D].reshape(3 * TILE, D))
                 me.Wq[layer, :, :, :, :, :, j : j + D] = d_qkv.astype(BF).reshape(n_z, 2, 2, 2, 16, D)
@@ -1102,8 +1110,8 @@
             add_bias(layer, B_V, rows_sum(value))
             me.GL[tile, :, D : 2 * D] = key.astype(BF)
             me.GL[tile, :, 2 * D :] = value.astype(BF)
-        third_y.wait_recv()
-        third = me.OWN[...] + me.RB2[...].astype(F32)
+        third_y.wait()
+        third = [me.OWN[i] + me.RB2[:, D * i : D * i + D].astype(F32) for i in range(2)]
         me.GL[2, :, D : 2 * D] = third[0].astype(BF)
         me.GL[2, :, 2 * D :] = third[1].astype(BF)
         add_bias(layer, B_V, rows_sum(third[1]))
@@ -1237,9 +1245,9 @@
             pltpu.VMEM((3, TILE, 3 * D), BF),
             pltpu.VMEM((2, 4 * TILE, D), F32),
             pltpu.VMEM((2, TILE, D), F32),
-            pltpu.VMEM((2, 3, TILE, D), BF),
             pltpu.VMEM((2, 2, TILE, D), BF),
-            pltpu.VMEM((2, TILE, D), BF),
+            pltpu.VMEM((2, 2, TILE, D), BF),
+            pltpu.VMEM((TILE, 2 * D), BF),
             pltpu.VMEM((2, TILE, 2 * D), BF),
         ]
         + many((n_z, 2, 2))
@@ -1279,7 +1287,7 @@
     )(*operands)
 
 
-VMEM_BYTES = 127 * 512 * 1024
+VMEM_BYTES = 67_000_000
 
 
 def fused_body(
@@ -1289,10 +1297,32 @@
         lax.axis_size("dp") // 2, timesteps, importance, jnp.swapaxes(inputs, 0, 1), jnp.swapaxes(cotangent, 0, 1),
         w_qkv, w_out, w_up, w_down, norm_gains, biases, jnp.swapaxes(time_table, 1, 2),
     )
-    return (
-        jnp.swapaxes(act, 0, 1).astype(F32), jnp.swapaxes(grad_in, 0, 1).astype(F32), g_qkv, g_out, g_up, g_down,
-        grad_gains, grad_biases, jnp.swapaxes(grad_table, 1, 2),
-    )
+    act, grad_in, *rest = finish_call((act, grad_in), (g_qkv, g_out, g_up, g_down, grad_gains, grad_biases, grad_table))
+    return (jnp.swapaxes(act, 0, 1), jnp.swapaxes(grad_in, 0, 1), *rest[:-1], jnp.swapaxes(rest[-1], 1, 2))
+
+
+def finish_kernel(n_wide, n_same, *refs):
+    ins, outs = refs[: n_wide + n_same], refs[n_wide + n_same :]
+    for source, target in zip(ins[:n_wide], outs[:n_wide]):
+        target[...] = source[...].astype(F32)
+
+    def hand_on():
+        for source, target in zip(ins[n_wide:], outs[n_wide:]):
+            target[...] = source[...]
+
+    pl.when(pl.program_id(0) == 0)(hand_on)
+
+
+def finish_call(wide, same):
+    tile = pl.BlockSpec((1, TILE, D), lambda i: (i, 0, 0))
+    whole = [pl.BlockSpec(array.shape, lambda i, rank=array.ndim: (0,) * rank) for array in same]
+    return pl.pallas_call(
+        functools.partial(finish_kernel, len(wide), len(same)),
+        grid=(3,),
+        out_shape=[jax.ShapeDtypeStruct(array.shape, F32) for array in (*wide, *same)],
+        in_specs=[tile] * len(wide) + whole,
+        out_specs=[tile] * len(wide) + whole,
+    )(*wide, *same)
 
 
 def solution(mesh):

time: 217 us -> 209 us (0.963)
  local copies, waits for them, and re-layouts: 4.54 us -> 0 us
  other arithmetic: 3.53 us -> 0 us
    unnamed x21 -> x0, local copies, waits for them, and re-layouts: 4.54 us -> none
    pallas_call x0 -> x1, Pallas kernels: none -> 4.3 us  [finish_call(): pl.pallas_call(functools.partial(finish_kernel, len(wide), len(same)), gr...]
    pallas_call x1, Pallas kernels: 204 us -> 200 us  [fused_call(): pl.pallas_call(run, out_shape=outs, in_specs=[smem, smem] + [any_space] *...]
    convert_element_type x1 -> x0, other arithmetic: 3.53 us -> none  [fused_body(): jnp.swapaxes(grad_in, 0, 1).astype(F32)]
where the time goes in v1:
time: 209 us; the launch traced here: 205 us
  Pallas kernels  204 us (98%)
    pallas_call x1, Pallas kernels, fused_call(): pl.pallas_call(run, out_shape=outs, in_specs=[smem, smem] + [any_space] *...  200 us
    pallas_call x1, Pallas kernels, finish_call(): pl.pallas_call(functools.partial(finish_kernel, len(wide), len(same)), gr...  4.3 us

profile of v1, /device:TPU:0, one launch (start us, length us, event | category | flops | bytes accessed | tf_op | source)
XLA Modules:
  0.0 205.3 jit_solution(12309213847522201014)
XLA Ops:
  0.6 200.1 %shard_map.178 = (bf16[3,256,512]{2,1,0:T(8,128)(2,1)}, bf16[3,256,512]{2,1,0:T(8,128)(2,1)}, f32[2,16,1536]{2,1,0:T(8,128)}, f32[2,16,512]{2,1,0:T(8,128)}, f32...) custom-call(s32[3]{0:T(128)} %refs_0_.1, ...), custom_call_target="tpu_custom_call" | custom-call | tf_op jit(solution)/shard_map/pallas_call | solution.py:1280
  200.8 4.3 %shard_map.179 = (f32[3,256,512]{2,1,0:T(8,128)}, f32[3,256,512]{2,1,0:T(8,128)}, f32[2,16,1536]{2,1,0:T(8,128)}, f32[2,16,512]{2,1,0:T(8,128)}, f32[2,16,2048]{...) custom-call(bf16[3,256,512]{2,1,0:T(8,128)(2,1)} %get-tuple-element.27.refs, ...), custom_call_target="tpu_custom_call" | custom-call | tf_op jit(solution)/shard_map/pallas_call | solution.py:1319

commit v2 on v1

--- a/solution.py
+++ b/solution.py
@@ -589,53 +589,54 @@
 BACKWARD_AT = (21, 0)
 END_AT = 42
 GATHER = (
-    ("yzxc", 0, 2, 3, 4),
-    ("zpc", 0, 2, 4),
-    ("zpc", 0, 3, 6),
-    ("yzxc", 0, 2, 3, 6),
-    ("pzc", 2, 4, 14),
-    ("zpc", 1, 5, 10),
-    ("zpc", 2, 7, 14),
-    ("zpc", 2, 9, 18),
+    ("pzc", 5, 6, 11),
+    ("pzc", 0, 5, 11),
     ("zpc", 0, 3, 11),
-    ("pzc", 1, 3, 12),
-    ("zpc", 3, 16, 21),
-    ("zpc", 6, 17, 21),
-    ("zpc", 2, 20, 32),
-    ("zpc", 7, 22, 32),
-    ("yzxc", 2, 8, 21, 32),
-    ("pzc", 1, 10, 28),
-    ("pzc", 17, 22, 33),
-    ("zpc", 8, 23, 32),
-    ("zpc", 0, 2, 5),
+    ("zpc", 0, 4, 10),
+    ("pzc", 0, 10, 20),
+    ("zpc", 0, 5, 19),
+    ("zpc", 6, 14, 20),
+    ("zpc", 11, 15, 23),
+    ("zyxc", 0, 5, 8, 17),
+    ("zpc", 4, 7, 21),
+    ("pzc", 8, 15, 25),
+    ("zpc", 12, 15, 25),
+    ("zpc", 1, 18, 31),
+    ("zpc", 12, 18, 37),
+    ("zpc", 13, 22, 33),
+    ("pzc", 8, 15, 34),
+    ("zpc", 12, 28, 38),
+    ("pzc", 21, 28, 38),
+    ("pzc", 0, 4, 6),
+    ("zpc", 2, 5, 7),
     ("y", 0),
-    ("y", 23),
+    ("y", 33),
 )
 REDUCE = (
-    ("cxzy", 9, 11, 15, 28, 43),
-    ("cxyz", 9, 12, 21, 35, 41),
-    ("cpz", 2, 5, 12, 15),
-    ("cpz", 4, 7, 13, 32),
-    ("cpz", 6, 14, 24, 37),
-    ("cpz", 7, 15, 29, 34),
-    ("cpz", 15, 20, 29, 40),
-    ("cpz", 15, 15, 32, 40),
-    ("cpz", 17, 22, 33, 40),
-    ("cpz", 18, 21, 33, 36),
-    ("cxzy", 28, 30, 36, 44, 44),
-    ("cxyz", 29, 32, 36, 42, 44),
-    ("cpz", 23, 24, 33, 44),
-    ("cpz", 25, 27, 33, 43),
-    ("cpz", 27, 30, 41, 45),
-    ("cpz", 28, 30, 39, 42),
-    ("cpz", 36, 38, 42, 46),
-    ("cpz", 36, 36, 41, 42),
+    ("cpz", 10, 15, 26, 32),
+    ("cxzy", 5, 12, 18, 26, 42),
+    ("cpz", 2, 6, 14, 32),
+    ("cxzy", 8, 11, 15, 31, 43),
+    ("cpz", 6, 10, 12, 40),
+    ("cpz", 11, 12, 32, 42),
+    ("cpz", 15, 15, 23, 40),
+    ("cpz", 15, 15, 32, 34),
+    ("cpz", 21, 24, 32, 35),
+    ("cpz", 17, 21, 33, 41),
+    ("cpz", 26, 28, 33, 42),
+    ("cxzy", 30, 33, 36, 44, 46),
+    ("cpz", 23, 25, 35, 43),
+    ("cxzy", 28, 31, 34, 44, 46),
+    ("cpz", 32, 36, 42, 44),
+    ("cpz", 29, 35, 44, 46),
+    ("cpz", 36, 37, 42, 44),
+    ("cpz", 36, 36, 39, 43),
     ("cpz", 38, 38, 42, 44),
-    ("cpz", 38, 40, 43, 46),
-    ("y", 41),
+    ("cpz", 38, 38, 42, 44),
+    ("y", 40),
 )
 
-SMALL = "small"
+SMALL, TIMES = "small", "times"
 
 
 def pieces(name, layer):
@@ -697,7 +698,6 @@
     grads = {"q": me.Wq, "o": me.Wo, "u": me.Wu, "d": me.Wd}
 
     steps_all = Gather(me, lambda gz, gx, gy, gc: me.TT.at[gz, gx], "d")
-    times = Gather(me, lambda *where: me.TS.at[where], "zpc")
     token_in = me.remote(me.xin.at[me.other["y"]], me.DO.at[1], "y")
     cot_in = me.remote(me.cot.at[me.other["y"]], me.GB.at[1], "y")
     moves = {}
@@ -708,6 +708,7 @@
             for part in range(pieces(name, layer)):
                 moves[name, part, layer] = weight(layer, ref, next(plan)[0], slice(width * part, width * (part + 1)))
     moves[SMALL] = small = Gather(me, lambda *where: me.SM.at[where], next(plan)[0])
+    moves[TIMES] = times = Gather(me, lambda *where: me.TS.at[where], next(plan)[0])
     timeline = by_place([*moves.values(), Single(token_in), Single(cot_in)], GATHER)
 
     def have(names, layer):
@@ -731,13 +732,8 @@
     hot = (t24[:, 0:1] == lax.broadcasted_iota(jnp.int32, (32, STEPS), 1)).astype(F32).astype(BF)
     picked = jnp.concatenate([nt(hot, me.tab[layer])[:24] for layer in range(LAYERS)], axis=0).astype(BF)
     me.TS[z, x, y, c] = nn(picked, own_lanes.astype(BF)).astype(BF)
-    times.start(0)
-    fire(2)
-    times.start(1)
-    fire(3)
-    times.start(2)
-    fire(4)
-    fire(5)
+    for place in range(2, 11):
+        fire(place)
 
     small.arrive()
     for gz in range(n_z):
@@ -897,21 +893,21 @@
         on_c[layer].wait_recv()
 
     announce(0)
-    fire(6)
+    fire(11)
     have("q", 0)
     project(0, 2)
-    fire(7)
+    fire(12)
     project(0, 0)
-    fire(8)
+    fire(13)
     token_in.wait_recv()
     me.X[0, 1] = me.DO[1].astype(F32) + time_row(0, 1)
     project(0, 1)
-    fire(9)
+    fire(14)
     neighbour(0)
     to_c[0][0].wait_recv()
     to_c[0][1].wait_recv()
     for layer in range(LAYERS):
-        at = (10, 25)[layer]
+        at = (15, 30)[layer]
         attention(layer, 0, 4, at)
         fire(at + 4)
         if layer:
@@ -924,11 +920,11 @@
             for tile in range(3):
                 me.X[1, tile] = me.GN[tile] + time_row(1, tile)
             announce(1)
-            fire(21)
+            fire(26)
             have("q", 1)
             for turn, tile in enumerate((2, 0, 1)):
                 project(1, tile)
-                fire(22 + turn)
+                fire(27 + turn)
             to_c[1][0].wait_recv()
             to_c[1][1].wait_recv()
     act_out = [
@@ -944,7 +940,7 @@
     for tile in range(3):
         grad = me.GB[tile].astype(F32) * (weight_2 if tile == 2 else weight_y)
         me.G[tile] = grad
-    for part in [steps_all, times, *moves.values()]:
+    for part in [steps_all, *moves.values()]:
         part.drain()
     for copy in sends:
         copy.wait_send()
@@ -1026,10 +1022,9 @@
         fire(base + 5)
         before_out()
         w_out = me.Wo[layer].reshape(D, D)
+        me.DO[...] = nt(me.GB[...].reshape(3 * TILE, D), w_out).astype(BF).reshape(3, TILE, D)
         for tile in range(3):
-            grad_attn = nt(me.GB[tile], w_out).astype(BF)
-            me.DO[tile] = grad_attn
-            delta = nt(selector, grad_attn.astype(F32) * me.AO[layer, tile].astype(F32), lax.Precision.HIGHEST)
+            delta = nt(selector, me.DO[tile].astype(F32) * me.AO[layer, tile].astype(F32), lax.Precision.HIGHEST)
             for pair in range(PAIRS):
                 both = jnp.concatenate([delta[2 * pair : 2 * pair + 1], delta[2 * pair + 1 : 2 * pair + 2]], axis=1)
                 me.DL[tile, pair] = both

time: 209 us -> 205 us (0.981)
  Pallas kernels: 204 us -> 201 us
    pallas_call x1, Pallas kernels: 200 us -> 197 us  [fused_call(): pl.pallas_call(run, out_shape=outs, in_specs=[smem, smem] + [any_space] *...]
where the time goes in v2:
time: 205 us; the launch traced here: 202 us
  Pallas kernels  201 us (98%)
    pallas_call x1, Pallas kernels, fused_call(): pl.pallas_call(run, out_shape=outs, in_specs=[smem, smem] + [any_space] *...  197 us
    pallas_call x1, Pallas kernels, finish_call(): pl.pallas_call(functools.partial(finish_kernel, len(wide), len(same)), gr...  4.3 us

profile of v2, /device:TPU:0, one launch (start us, length us, event | category | flops | bytes accessed | tf_op | source)
XLA Modules:
  0.0 201.7 jit_solution(14624232121958669401)
XLA Ops:
  0.6 196.6 %shard_map.178 = (bf16[3,256,512]{2,1,0:T(8,128)(2,1)}, bf16[3,256,512]{2,1,0:T(8,128)(2,1)}, f32[2,16,1536]{2,1,0:T(8,128)}, f32[2,16,512]{2,1,0:T(8,128)}, f32...) custom-call(s32[3]{0:T(128)} %refs_0_.1, ...), custom_call_target="tpu_custom_call" | custom-call | tf_op jit(solution)/shard_map/pallas_call | solution.py:1275
  197.2 4.3 %shard_map.179 = (f32[3,256,512]{2,1,0:T(8,128)}, f32[3,256,512]{2,1,0:T(8,128)}, f32[2,16,1536]{2,1,0:T(8,128)}, f32[2,16,512]{2,1,0:T(8,128)}, f32[2,16,2048]{...) custom-call(bf16[3,256,512]{2,1,0:T(8,128)(2,1)} %get-tuple-element.27.refs, ...), custom_call_target="tpu_custom_call" | custom-call | tf_op jit(solution)/shard_map/pallas_call | solution.py:1314

commit v3 on v2

--- a/solution.py
+++ b/solution.py
@@ -631,8 +631,8 @@
     ("cpz", 29, 35, 44, 46),
     ("cpz", 36, 37, 42, 44),
     ("cpz", 36, 36, 39, 43),
-    ("cpz", 38, 38, 42, 44),
-    ("cpz", 38, 38, 42, 44),
+    ("cpz", 37.25, 38, 42, 44),
+    ("cpz", 37.5, 38, 42, 44),
     ("y", 40),
 )
 
@@ -1111,7 +1111,10 @@
         me.GL[2, :, 2 * D :] = third[1].astype(BF)
         add_bias(layer, B_V, rows_sum(third[1]))
         fire(base + 16)
-        qkv_back(D, 3 * D)
+        qkv_back(D, 2 * D)
+        fire(base + 16.25)
+        qkv_back(2 * D, 3 * D)
+        fire(base + 16.5)
         fire(base + 17)
         totals = []
         for tile in (1, 0, 2):

time: 205 us -> 205 us (level)
  no operation moved by 1% of the time
where the time goes in v3:
time: 205 us; the launch traced here: 201 us
  Pallas kernels  200 us (98%)
    pallas_call x1, Pallas kernels, fused_call(): pl.pallas_call(run, out_shape=outs, in_specs=[smem, smem] + [any_space] *...  196 us
    pallas_call x1, Pallas kernels, finish_call(): pl.pallas_call(functools.partial(finish_kernel, len(wide), len(same)), gr...  4.3 us

profile of v3, /device:TPU:0, one launch (start us, length us, event | category | flops | bytes accessed | tf_op | source)
XLA Modules:
  0.0 201.1 jit_solution(15885870006033085923)
XLA Ops:
  0.6 195.9 %shard_map.178 = (bf16[3,256,512]{2,1,0:T(8,128)(2,1)}, bf16[3,256,512]{2,1,0:T(8,128)(2,1)}, f32[2,16,1536]{2,1,0:T(8,128)}, f32[2,16,512]{2,1,0:T(8,128)}, f32...) custom-call(s32[3]{0:T(128)} %refs_0_.1, ...), custom_call_target="tpu_custom_call" | custom-call | tf_op jit(solution)/shard_map/pallas_call | solution.py:1278
  196.6 4.3 %shard_map.179 = (f32[3,256,512]{2,1,0:T(8,128)}, f32[3,256,512]{2,1,0:T(8,128)}, f32[2,16,1536]{2,1,0:T(8,128)}, f32[2,16,512]{2,1,0:T(8,128)}, f32[2,16,2048]{...) custom-call(bf16[3,256,512]{2,1,0:T(8,128)(2,1)} %get-tuple-element.27.refs, ...), custom_call_target="tpu_custom_call" | custom-call | tf_op jit(solution)/shard_map/pallas_call | solution.py:1317
